TPU v7x, 32 devices: a whole 2x2x4 slice. The times are simulated.
32 devices in a mesh: groups: 2 (over y), dp: 8 (over z, core), vocab: 2 (over x).
Axes of the slice: x: 2, y: 2, z: 4, core: 2. Of those that a mesh axis runs over, the one named last changes fastest.
Arguments:
- teacher_hidden: bfloat16 [128, 5120], P(('groups', 'dp')), parts along dimension 0, may hold values from -110 to 110
- teacher_head: bfloat16 [5120, 98304], P(None, ('dp', 'vocab')), may hold values from -0.078125 to 0.078125
- map_dest: int32 [768, 4], P(('dp', 'vocab')), may hold values from 0 to 7, all different within a row; in each aligned block of 48 rows (0 to 47, 48 to 95, ...) at most 24 rows name the same one
- map_slot: int32 [768, 4], P(('dp', 'vocab')), may hold values from 0 to 31
- map_weight: bfloat16 [768, 4, 128, 128], P(('dp', 'vocab')), may hold values from 0.019897461 to 1
- student_hidden: bfloat16 [128, 4096], P(('groups', 'dp')), parts along dimension 0, may hold values from -110 to 110
- student_head: bfloat16 [4096, 65536], P(None, ('dp', 'vocab')), may hold values from -0.09375 to 0.09375
- targets: int32 [128], P(('groups', 'dp')), parts along dimension 0, may hold values from 0 to 65535
Outputs:
- grad_hidden: bfloat16 [128, 4096], P(('groups', 'dp', 'vocab')), parts along dimension 0
There are 2 independent parts, one for each index of `groups`. A program takes and returns all parts, laid end to end along the dimension named above; an argument that names none is the same for every part. Nothing has to cross between parts.
Inputs may be any that keep to these rules, and one draw needn't show every extreme that they name: `map_dest`: the 4 entries of a row differ. Among the 48 rows of one device (aligned blocks of rows) no value appears more than 24 times, and some value appears exactly 24 times.
All inputs are finite; a program needn't handle non-finite values.
Results may differ from a plain program's by a relative error of at most 0.012.
Values may be sent and summed in bfloat16 or wider, within the bound.
A program may use at most 192 MiB of HBM per device.

v0:
```python
import jax
import jax.numpy as jnp
from jax import lax
from jax.sharding import PartitionSpec as P

hard_weight = 0.25
loss_scale = 64.0


def on_device(
    teacher_hidden,
    teacher_head,
    map_dest,
    map_slot,
    map_weight,
    student_hidden,
    student_head,
    targets,
):
    dp_count = lax.axis_size("dp")
    vocab_count = lax.axis_size("vocab")
    block_size = map_weight.shape[2]
    teacher_blocks = map_dest.shape[0]
    fan_count = map_dest.shape[1]
    student_cols = student_head.shape[1]
    student_blocks = student_cols // block_size
    capacity = max(2, (teacher_blocks * fan_count + dp_count - 1) // dp_count)
    device_flat = lax.axis_index("dp") * vocab_count + lax.axis_index("vocab")
    teacher_logits = jnp.dot(
        lax.all_gather(teacher_hidden, "dp", axis=0, tiled=True),
        teacher_head,
        preferred_element_type=jnp.float32,
    )
    student_logits = jnp.dot(
        lax.all_gather(student_hidden, "dp", axis=0, tiled=True),
        student_head,
        preferred_element_type=jnp.float32,
    )
    all_targets = lax.all_gather(targets, "dp", axis=0, tiled=True)
    tokens_all = teacher_logits.shape[0]
    teacher_peak = lax.pmax(jnp.max(teacher_logits, axis=1), ("dp", "vocab"))
    teacher_exp = jnp.exp(teacher_logits - teacher_peak[:, None])
    student_peak = lax.pmax(jnp.max(student_logits, axis=1), ("dp", "vocab"))
    student_total = lax.psum(
        jnp.sum(jnp.exp(student_logits - student_peak[:, None]), axis=1), ("dp", "vocab")
    )
    teacher_weights = teacher_exp.astype(jnp.bfloat16)
    prob_blocks = teacher_weights.reshape(tokens_all, teacher_blocks, block_size)
    mapped_terms = jnp.einsum(
        "gkc,krcd->krgd", prob_blocks, map_weight, preferred_element_type=jnp.float32
    ).astype(jnp.bfloat16)
    item_count = teacher_blocks * fan_count
    dest_flat = map_dest.reshape(item_count)
    dest_onehot = (dest_flat[:, None] == jnp.arange(dp_count, dtype=jnp.int32)[None, :]).astype(
        jnp.int32
    )
    earlier_same = jnp.sum(jnp.cumsum(dest_onehot, axis=0) * dest_onehot, axis=1) - 1
    slot_index = dest_flat * capacity + earlier_same
    placement = (
        jnp.arange(dp_count * capacity, dtype=jnp.int32)[:, None] == slot_index[None, :]
    ).astype(jnp.bfloat16)
    outgoing = jnp.dot(
        placement,
        mapped_terms.reshape(item_count, tokens_all * block_size),
        preferred_element_type=jnp.float32,
    )
    outgoing = outgoing.astype(jnp.bfloat16).reshape(dp_count, capacity, tokens_all, block_size)
    slot_onehot = (
        map_slot.reshape(item_count)[:, None]
        == jnp.arange(student_blocks, dtype=jnp.int32)[None, :]
    ).astype(jnp.bfloat16)
    slot_marks = jnp.dot(placement, slot_onehot, preferred_element_type=jnp.float32).astype(
        jnp.bfloat16
    )
    slot_marks = slot_marks.reshape(dp_count, capacity, student_blocks)
    incoming, marks_in = (
        lax.all_to_all(outgoing, "dp", split_axis=0, concat_axis=0, tiled=True),
        lax.all_to_all(slot_marks, "dp", split_axis=0, concat_axis=0, tiled=True),
    )
    mapped = jnp.dot(
        marks_in.reshape(dp_count * capacity, student_blocks).T,
        incoming.reshape(dp_count * capacity, tokens_all * block_size),
        preferred_element_type=jnp.float32,
    )
    mapped = jnp.transpose(
        mapped.reshape(student_blocks, tokens_all, block_size), (1, 0, 2)
    ).reshape(tokens_all, student_cols)
    target_total = lax.psum(jnp.sum(mapped, axis=1), ("dp", "vocab"))
    target_probs = mapped / target_total[:, None]
    student_probs = jnp.exp(student_logits - student_peak[:, None]) / student_total[:, None]
    columns = device_flat * student_cols + jnp.arange(student_cols, dtype=jnp.int32)
    target_hits = (all_targets[:, None] == columns[None, :]).astype(jnp.float32)
    logit_grad = (
        loss_scale
        * (student_probs - (1.0 - hard_weight) * target_probs - hard_weight * target_hits)
    ).astype(jnp.bfloat16)
    gradient = lax.psum_scatter(
        lax.dot_general(
            logit_grad, student_head, (((1,), (1,)), ((), ())), preferred_element_type=jnp.float32
        ),
        ("dp", "vocab"),
        scatter_dimension=0,
        tiled=True,
    )
    return gradient.astype(jnp.bfloat16)


def solution(mesh):
    placed = (
        P(("groups", "dp"), None),
        P(None, ("dp", "vocab")),
        P(("dp", "vocab"), None),
        P(("dp", "vocab"), None),
        P(("dp", "vocab"), None, None, None),
        P(("groups", "dp"), None),
        P(None, ("dp", "vocab")),
        P(("groups", "dp")),
    )
    return jax.shard_map(
        on_device,
        mesh=mesh,
        in_specs=placed,
        out_specs=P(("groups", "dp", "vocab"), None),
        check_vma=False,
    )
```

profile of v0, /device:TPU:0, one launch (start us, length us, event | category | flops | bytes accessed | tf_op | source)
XLA Modules:
  0.0 323.9 jit_solution(15093153480868843150)
XLA Ops:
  0.0 0.8 copy.14
  0.8 0.1 reshape.57
  0.9 0.6 reduce-window.6
  1.5 0.2 slice_reduce_fusion
  1.9 0.8 copy.15
  2.6 0.1 eq.70
  2.7 0.3 convolution_convert_fusion.2
  3.0 0.1 copy.21
  3.1 0.7 reshape.77
  3.8 6.3 %all-to-all-start = ((bf16[8,2,384]{2,1,0:T(2,128)(2,1)}), bf16[8,2,384]{2,1,0:T(2,128)(2,1)S(1)}, u32[]{:S(2)}, u32[]{:S(2)}) async-start(bf16[8,2,384]{2,1,0:T(2,128)(2,1)} %reshape.77), calls=%async_computation | async-start | bytes 24576 | tf_op jit(solution)/shard_map/all_to_all | solution.py:78
  10.2 15.8 %all_gather.10 = bf16[64,5120]{1,0:T(8,128)(2,1)S(1)} all-gather(bf16[8,5120]{1,0:T(8,128)(2,1)} %param.8), channel_id=1, replica_groups=mesh['groups'=2,'dp'=8,'vocab'=2] {'dp'}, dimensions={0}, use_global_device_ids=true | all-gather | bytes 737280 | tf_op jit(solution)/shard_map/all_gather | solution.py:30
  25.9 15.2 %all_gather.9 = bf16[64,4096]{1,0:T(8,128)(2,1)S(1)} all-gather(bf16[8,4096]{1,0:T(8,128)(2,1)} %param.13), channel_id=1, replica_groups=mesh['groups'=2,'dp'=8,'vocab'=2] {'dp'}, dimensions={0}, use_global_device_ids=true | all-gather | bytes 589824 | tf_op jit(solution)/shard_map/all_gather | solution.py:35
  41.1 23.0 %fusion.35 = (f32[64]{0:T(128)S(1)}, f32[64,6144]{1,0:T(8,128)S(1)}) fusion(bf16[64,5120]{1,0:T(8,128)(2,1)S(1)} %all_gather.10, bf16[5120,6144]{1,0:T(8,128)(2,1)} %param.9), kind=kOutput, calls=%fused_computation.50 | convolution fusion | flops 4026925056 | bytes 65143040 | tf_op jit(solution)/shard_map/dot_general | solution.py:29
  64.2 13.7 %fusion.36 = (f32[64]{0:T(128)S(1)}, f32[64,4096]{1,0:T(8,128)S(1)}) fusion(bf16[64,4096]{1,0:T(8,128)(2,1)S(1)} %all_gather.9, bf16[4096,4096]{1,0:T(8,128)(2,1)} %param.14), kind=kOutput, calls=%fused_computation.51 | convolution fusion | flops 2147745792 | bytes 35127552 | tf_op jit(solution)/shard_map/dot_general | solution.py:34
  77.9 34.2 %all-reduce.4 = (f32[64]{0:T(128)S(1)}, f32[64]{0:T(128)S(1)}) all-reduce(f32[64]{0:T(128)S(1)} %get-tuple-element.9, f32[64]{0:T(128)S(1)} %get-tuple-element.11), channel_id=1, replica_groups=mesh['groups'=2,'dp'=8,'vocab'=2] {'dp','vocab'}, use_global_device_ids=true, to_apply=%region_8.9 | all-reduce | flops 128 | bytes 1024 | tf_op jit(solution)/shard_map/pmax | solution.py:41
  112.1 0.3 fusion.14
  112.3 0.1 copy.26
  112.5 3.8 %convolution_convert_fusion.1 = bf16[48,64,4,128]{3,1,2,0:T(8,128)(2,1)S(1)} fusion(bf16[48,4,128,128]{3,2,1,0:T(8,128)(2,1)} %param.12, bf16[64,48,128,1]{2,1,0,3:T(8,128)(2,1)S(1)} %bitcast.69), kind=kOutput, calls=%fused_computation.7 | convolution fusion | flops 404226048 | bytes 10223616 | tf_op jit(solution)/shard_map/gkc,krcd->krgd/dot_general | solution.py:49
  116.3 2.4 fusion.5
  118.6 2.6 copy.28
  121.3 4.6 %all-to-all-start.1 = ((bf16[8,24,64,128]{3,2,1,0:T(8,128)(2,1)}), bf16[8,24,64,128]{3,2,1,0:T(8,128)(2,1)}, u32[]{:S(2)}, u32[]{:S(2)}) async-start(bf16[8,24,64,128]{3,2,1,0:T(8,128)(2,1)} %bitcast.24), calls=%async_computation.1 | async-start | bytes 6291456 | tf_op jit(solution)/shard_map/all_to_all | solution.py:77
  125.9 0.6 dynamic-slice
  127.1 0.6 dynamic-slice.1
  128.3 0.2 dynamic-update-slice
  128.6 69.0 %all-reduce.1 = s32[64]{0:T(128)S(1)} all-reduce(s32[64]{0:T(128)S(1)} %dynamic-update-slice), channel_id=1, replica_groups=mesh['groups'=2,'dp'=8,'vocab'=2] {'dp'}, use_global_device_ids=true, to_apply=%add.1 | all-reduce | flops 64 | bytes 512
  197.5 0.3 fusion.13
  197.9 0.1 reshape.78
  198.0 4.0 %fusion.37 = (f32[64]{0:T(128)S(1)}, f32[32,64,128]{2,0,1:T(8,128)S(1)}) fusion(bf16[192,32,1]{1,0,2:T(8,128)(2,1)S(1)} %bitcast.72, bf16[24,8,64,128]{3,2,1,0:T(8,128)(2,1)} %bitcast.26), kind=kOutput, calls=%fused_computation.52 | convolution fusion | flops 100925376 | bytes 4206848 | tf_op jit(solution)/shard_map/dot_general | solution.py:80
  201.9 29.5 %all-reduce.3 = (f32[64]{0:T(128)S(1)}, f32[64]{0:T(128)S(1)}) all-reduce(f32[64]{0:T(128)S(1)} %get-tuple-element.13, f32[64]{0:T(128)S(1)} %fusion.13), channel_id=1, replica_groups=mesh['groups'=2,'dp'=8,'vocab'=2] {'dp','vocab'}, use_global_device_ids=true, to_apply=%region_10.11 | all-reduce | flops 128 | bytes 1024 | tf_op jit(solution)/shard_map/psum | solution.py:88
  231.4 16.1 %fusion.16 = f32[64,4096]{1,0:T(8,128)S(1)} fusion(bf16[4096,4096]{1,0:T(8,128)(2,1)} %param.14, f32[8,8,32,128]{3,2,1,0:T(8,128)S(1)} %bitcast.70, f32[64,4096]{1,0:T(8,128)S(1)} %get-tuple-element.12, s32[4096]{0:T(1024)S(1)} %iota_add_fusion, f32[64]{0:T(128)S(1)} %get-tuple-element.5, f32[64]{0:T(128)S(1)} %get-tuple-element.6, ...), kind=kOutput, calls=%fused_computation.21 | convolution fusion | flops 2150105088 | bytes 36717568 | tf_op jit(solution)/shard_map/dot_general | solution.py:98
  247.5 75.7 %all-reduce.6 = bf16[64,4096]{1,0:T(8,128)(2,1)S(1)} all-reduce(f32[64,4096]{1,0:T(8,128)S(1)} %fusion.16), channel_id=2, replica_groups=mesh['groups'=2,'dp'=8,'vocab'=2] {'dp','vocab'}, use_global_device_ids=true, to_apply=%region_11.12.clone | all-reduce | flops 262144 | bytes 1572864
  323.2 0.6 dynamic-slice_convert_fusion
  (17 shorter events, 0.2 us)
Async XLA Ops:
  3.8 117.4 %all-to-all-start = ((bf16[8,2,384]{2,1,0:T(2,128)(2,1)}), bf16[8,2,384]{2,1,0:T(2,128)(2,1)S(1)}, u32[]{:S(2)}, u32[]{:S(2)}) async-start(bf16[8,2,384]{2,1,0:T(2,128)(2,1)} %reshape.77), calls=%async_computation | async-start | bytes 24576 | tf_op jit(solution)/shard_map/all_to_all | solution.py:78
  121.3 4.6 %copy-start.2 = (u32[32]{0:T(128)S(1)}, u32[32]{0:T(128)}, u32[]{:S(2)}) copy-start(u32[32]{0:T(128)} %constant.43) | copy-start | bytes 388
  121.3 5.9 %copy-start.1 = (u32[32]{0:T(128)S(1)}, u32[32]{0:T(128)}, u32[]{:S(2)}) copy-start(u32[32]{0:T(128)} %constant.49) | copy-start | bytes 388
  121.3 7.1 %copy-start = (s32[8]{0:T(128)S(1)}, s32[8]{0:T(128)}, u32[]{:S(2)}) copy-start(s32[8]{0:T(128)} %param.15) | copy-start | bytes 100
  121.3 76.7 %all-to-all-start.1 = ((bf16[8,24,64,128]{3,2,1,0:T(8,128)(2,1)}), bf16[8,24,64,128]{3,2,1,0:T(8,128)(2,1)}, u32[]{:S(2)}, u32[]{:S(2)}) async-start(bf16[8,24,64,128]{3,2,1,0:T(8,128)(2,1)} %bitcast.24), calls=%async_computation.1 | async-start | bytes 6291456 | tf_op jit(solution)/shard_map/all_to_all | solution.py:77
where the time goes:
time: 324 us
  blocking collectives  239 us (74%)
  matrix products  63.2 us (20%)
  starting transfers between devices  10.9 us (3%)
  local copies, waits for them, and re-layouts  7.67 us (2%)
    unnamed x2, blocking collectives  145 us
    pmax x1, blocking collectives, on_device(): teacher_peak = lax.pmax(jnp.max(teacher_logits, axis=1), ('dp', 'vocab'))  34.2 us
    psum x1, blocking collectives, on_device(): target_total = lax.psum(jnp.sum(mapped, axis=1), ('dp', 'vocab'))  29.5 us
    dot_general x1, matrix products, on_device(): jnp.dot(lax.all_gather(teacher_hidden, 'dp', axis=0, tiled=True), teacher...  23 us
    dot_general x1, matrix products, on_device(): lax.dot_general(logit_grad, student_head, (((1,), (1,)), ((), ())), prefe...  16.1 us
    all_gather x1, blocking collectives, on_device(): lax.all_gather(teacher_hidden, 'dp', axis=0, tiled=True)  15.8 us
    all_gather x1, blocking collectives, on_device(): lax.all_gather(student_hidden, 'dp', axis=0, tiled=True)  15.2 us
    dot_general x1, matrix products, on_device(): jnp.dot(lax.all_gather(student_hidden, 'dp', axis=0, tiled=True), student...  13.7 us
  transfers between devices with their start and end apart: 2, of which 0 were waited for; matrix products, arithmetic and copies ran while one was open for 15% of the time, Pallas kernels for 0%

commit v1 on v0

v1 whole, which is shorter than its diff:
```python
import functools

import jax
import jax.numpy as jnp
from jax import lax
from jax.experimental import pallas as pl
from jax.experimental.pallas import tpu as pltpu
from jax.sharding import PartitionSpec as P

MESH = pl.DeviceIdType.MESH
hard_weight = 0.25
loss_scale = 64.0
vmem_bytes = 60 * 1024 * 1024


def chunk_of(cols):
    for size in (512, 256, 128):
        if cols % size == 0:
            return size
    return cols


def teacher_kernel(
    chips, own_t, own_s, own_id, head, logits, all_s, all_id,
    held_t, held_s, held_id, tiles, tile_sem, send_sem, recv_sem, pass_sem, land_sem,
):
    place = lax.axis_index("dp")
    chip, core = place // 2, place % 2
    slots, width = tiles.shape[0], tiles.shape[2]
    steps = head.shape[1] // width

    def fetch(step, slot):
        return pltpu.make_async_copy(
            head.at[:, pl.ds(pl.multiple_of(step * width, width), width)],
            tiles.at[slot],
            tile_sem.at[slot],
        )

    for slot in range(min(slots, steps)):
        fetch(slot, slot).start()
    held_t[place] = own_t[...]
    held_s[place] = own_s[...]
    held_id[place] = own_id[...]

    barrier = pltpu.get_barrier_semaphore()
    partner = chip * 2 + (1 - core)
    for hop in range(1, chips):
        other = (chip + hop) % chips * 2 + core
        pl.semaphore_signal(barrier, inc=1, device_id={"dp": other}, device_id_type=MESH)
    pl.semaphore_signal(barrier, inc=1, device_id={"dp": partner}, device_id_type=MESH)
    pl.semaphore_wait(barrier, chips)

    helds = (held_t, held_id, held_s)

    def across(kind, hop):
        return pltpu.make_async_remote_copy(
            src_ref=helds[kind].at[place],
            dst_ref=helds[kind].at[place],
            send_sem=send_sem.at[kind, hop],
            recv_sem=recv_sem.at[kind, hop],
            device_id={"dp": (chip + hop) % chips * 2 + core},
            device_id_type=MESH,
        )

    def between(kind, hop):
        block = (chip + chips - hop) % chips * 2 + core
        return pltpu.make_async_remote_copy(
            src_ref=helds[kind].at[block],
            dst_ref=helds[kind].at[block],
            send_sem=pass_sem.at[kind, hop],
            recv_sem=land_sem.at[kind, hop],
            device_id={"dp": partner},
            device_id_type=MESH,
        )

    for kind in range(3):
        for hop in range(1, chips):
            across(kind, hop).start()
        between(kind, 0).start()
    for hop in range(1, chips):
        across(0, hop).wait_recv()
        between(0, hop).start()
    for hop in range(chips):
        between(0, hop).wait_recv()

    tokens = held_t.shape[0] * held_t.shape[1]

    def multiply(step, carry):
        slot = step % slots
        fetch(step, slot).wait()
        logits[:, pl.ds(pl.multiple_of(step * width, width), width)] = jnp.dot(
            held_t[...].reshape(tokens, held_t.shape[2]),
            tiles[slot],
            preferred_element_type=jnp.float32,
        )

        @pl.when(step + slots < steps)
        def _():
            fetch(step + slots, slot).start()

        return carry

    middle = steps // 2
    lax.fori_loop(0, middle, multiply, 0)
    for kind in (1, 2):
        for hop in range(1, chips):
            across(kind, hop).wait_recv()
            between(kind, hop).start()
    lax.fori_loop(middle, steps, multiply, 0)
    for kind in (1, 2):
        for hop in range(chips):
            between(kind, hop).wait_recv()
    for kind in range(3):
        for hop in range(1, chips):
            across(kind, hop).wait_send()
        for hop in range(chips):
            between(kind, hop).wait_send()
    all_s[...] = held_s[...]
    all_id[...] = held_id[...]


def teacher_call(chips, own_t, own_s, own_id, head):
    depth, cols = head.shape
    width = chunk_of(cols)
    slots = min(8, cols // width)
    places = chips * 2
    rows = own_t.shape[0]
    vmem = pl.BlockSpec(memory_space=pltpu.VMEM)
    return pl.pallas_call(
        functools.partial(teacher_kernel, chips),
        out_shape=(
            jax.ShapeDtypeStruct((places * rows, cols), jnp.float32),
            jax.ShapeDtypeStruct((places,) + own_s.shape, own_s.dtype),
            jax.ShapeDtypeStruct((places,) + own_id.shape, own_id.dtype),
        ),
        in_specs=[vmem, vmem, vmem, pl.BlockSpec(memory_space=pl.ANY)],
        out_specs=(vmem, vmem, vmem),
        scratch_shapes=[
            pltpu.VMEM((places,) + own_t.shape, own_t.dtype),
            pltpu.VMEM((places,) + own_s.shape, own_s.dtype),
            pltpu.VMEM((places,) + own_id.shape, own_id.dtype),
            pltpu.VMEM((slots, depth, width), head.dtype),
            pltpu.SemaphoreType.DMA((slots,)),
            pltpu.SemaphoreType.DMA((3, chips)),
            pltpu.SemaphoreType.DMA((3, chips)),
            pltpu.SemaphoreType.DMA((3, chips)),
            pltpu.SemaphoreType.DMA((3, chips)),
        ],
        compiler_params=pltpu.CompilerParams(
            collective_id=0, has_side_effects=True, vmem_limit_bytes=vmem_bytes
        ),
    )(own_t, own_s, own_id, head)


def student_kernel(
    chips, vocabs, dense, peak_row, all_s, all_id, head, out,
    whole, summed, up_in, down_in, peaks, stats, logits, grad, partial, sent, landed,
    tile_sem, peak_send, peak_recv, stat_send, stat_recv, core_send, core_recv,
    up_send, up_recv, down_send, down_recv, grad_send, grad_recv,
):
    place, vocab = lax.axis_index("dp"), lax.axis_index("vocab")
    chip, core = place // 2, place % 2
    partner = chip * 2 + (1 - core)
    count = chips * 2 * vocabs
    me = place * vocabs + vocab
    blocks, tokens, block = summed.shape[1:]
    depth, cols = head.shape
    width = chunk_of(cols)
    steps = cols // width
    last = chips - 1

    def fetch(step):
        at = pl.ds(pl.multiple_of(step * width, width), width)
        return pltpu.make_async_copy(head.at[:, at], whole.at[:, at], tile_sem.at[step])

    for step in range(steps):
        fetch(step).start()
    peaks[me] = peak_row[...]

    def every(body):
        lax.fori_loop(1, count, lambda hop, carry: (body(hop), carry)[1], 0)

    def peer(hop):
        other = (me + hop) % count
        return {"dp": other // vocabs, "vocab": other % vocabs}

    barrier = pltpu.get_barrier_semaphore()
    every(lambda hop: pl.semaphore_signal(barrier, inc=1, device_id=peer(hop), device_id_type=MESH))
    pl.semaphore_wait(barrier, count - 1)

    def share(ref, send_sem, recv_sem):
        def one(hop):
            return pltpu.make_async_remote_copy(
                src_ref=ref.at[me], dst_ref=ref.at[me],
                send_sem=send_sem.at[hop], recv_sem=recv_sem.at[hop],
                device_id=peer(hop), device_id_type=MESH,
            )
        return one

    share_peak = share(peaks, peak_send, peak_recv)
    share_stat = share(stats, stat_send, stat_recv)
    every(lambda hop: share_peak(hop).start())

    order = []
    for near in range((chips + 1) // 2):
        order += [last - near] + ([near] if near != last - near else [])

    def to_core(target):
        return pltpu.make_async_remote_copy(
            src_ref=dense.at[target * 2 + 1 - core], dst_ref=summed.at[target],
            send_sem=core_send.at[target], recv_sem=core_recv.at[target],
            device_id={"dp": partner}, device_id_type=MESH,
        )

    def up(target):
        return pltpu.make_async_remote_copy(
            src_ref=summed.at[target], dst_ref=up_in.at[target],
            send_sem=up_send.at[target], recv_sem=up_recv.at[target],
            device_id={"dp": (chip + 1) % chips * 2 + core}, device_id_type=MESH,
        )

    def down(target):
        return pltpu.make_async_remote_copy(
            src_ref=summed.at[target], dst_ref=down_in.at[target],
            send_sem=down_send.at[target], recv_sem=down_recv.at[target],
            device_id={"dp": (chip + last) % chips * 2 + core}, device_id_type=MESH,
        )

    for target in order:
        to_core(target).start()

    eye = lax.broadcasted_iota(jnp.int32, (tokens, tokens), 0) == lax.broadcasted_iota(
        jnp.int32, (tokens, tokens), 1
    )

    def column(row):
        return jnp.sum(jnp.where(eye, row, 0.0), axis=1, keepdims=True)

    def row_of(col):
        return jnp.sum(jnp.where(eye, col, 0.0), axis=0, keepdims=True)

    def add_rows(index, total):
        tile = dense[index // blocks, index % blocks]
        return total + tile.astype(jnp.float32)

    row_total = lax.fori_loop(
        0, 2 * chips * blocks, add_rows, jnp.zeros((tokens, block), jnp.float32)
    )
    every(lambda hop: share_peak(hop).wait())
    peak = column(jnp.max(peaks[:, 0:1, :], axis=0))
    own_scale = jnp.exp(column(peaks[me, 0:1, :]) - peak)
    partner_scale = jnp.exp(column(peaks[partner * vocabs + vocab, 0:1, :]) - peak)
    term_total = own_scale * jnp.sum(row_total, axis=1, keepdims=True)
    own_wide = jnp.broadcast_to(own_scale, (tokens, block))
    partner_wide = jnp.broadcast_to(partner_scale, (tokens, block))

    for target in order:
        to_core(target).wait_recv()

        def combine(index, carry):
            summed[target, index] = (
                dense[target * 2 + core, index].astype(jnp.float32) * own_wide
                + summed[target, index].astype(jnp.float32) * partner_wide
            ).astype(summed.dtype)
            return carry

        lax.fori_loop(0, blocks, combine, 0)
        if target > 0:
            @pl.when(chip == 0)
            def _():
                up(target).start()
        if target < last:
            @pl.when(chip == last)
            def _():
                down(target).start()

    def multiply(step, carry):
        fetch(step).wait()
        at = pl.ds(pl.multiple_of(step * width, width), width)
        logits[:, at] = jnp.dot(
            all_s[...].reshape(tokens, depth), whole[:, at], preferred_element_type=jnp.float32
        )
        return carry

    def add_in(target, ref):
        def one(index, carry):
            summed[target, index] = (
                summed[target, index].astype(jnp.float32) + ref[target, index].astype(jnp.float32)
            ).astype(summed.dtype)
            return carry

        lax.fori_loop(0, blocks, one, 0)

    done = 0
    for turn in range(last):
        until = steps if turn == last - 1 else min(steps, (steps + 1) // 2 + turn * (steps // 4))
        lax.fori_loop(done, until, multiply, 0)
        done = until
        high, low = last - turn, turn
        if high > 1:
            @pl.when((chip > 0) & (chip < high))
            def _():
                up(high).wait_recv()
                add_in(high, up_in)
                up(high).start()
        if low < last - 1:
            @pl.when((chip < last) & (chip > low))
            def _():
                down(low).wait_recv()
                add_in(low, down_in)
                down(low).start()

    own_peak = jnp.max(logits[...], axis=1, keepdims=True)
    own_sum = jnp.sum(jnp.exp(logits[...] - own_peak), axis=1, keepdims=True)
    stats[me, 0:1, :] = row_of(term_total)
    stats[me, 1:2, :] = row_of(own_peak)
    stats[me, 2:3, :] = row_of(own_sum)
    stats[me, 3:8, :] = jnp.zeros((5, tokens), jnp.float32)
    every(lambda hop: share_stat(hop).start())
    every(lambda hop: share_stat(hop).wait())
    target_total = column(jnp.sum(stats[:, 0:1, :], axis=0))
    student_peak_row = jnp.max(stats[:, 1:2, :], axis=0)
    student_total = column(
        jnp.sum(stats[:, 2:3, :] * jnp.exp(stats[:, 1:2, :] - student_peak_row), axis=0)
    )
    student_peak = column(student_peak_row)
    student_gain = jnp.broadcast_to(loss_scale / student_total, (tokens, block))
    target_gain = jnp.broadcast_to(loss_scale * (1.0 - hard_weight) / target_total, (tokens, block))
    peak_wide = jnp.broadcast_to(student_peak, (tokens, block))
    ids = all_id[...].reshape(tokens, block)
    lanes = lax.broadcasted_iota(jnp.int32, (tokens, block), 1) + me * cols

    for target in range(chips):
        if target > 0:
            @pl.when(chip == target)
            def _():
                up(target).wait_recv()
        if target < last:
            @pl.when(chip == target)
            def _():
                down(target).wait_recv()

    def finish(index, carry):
        mapped = summed[chip, index].astype(jnp.float32)
        mapped = mapped + jnp.where(chip > 0, up_in[chip, index].astype(jnp.float32), 0.0)
        mapped = mapped + jnp.where(chip < last, down_in[chip, index].astype(jnp.float32), 0.0)
        at = pl.ds(pl.multiple_of(index * block, block), block)
        student = jnp.exp(logits[:, at] - peak_wide) * student_gain
        hits = jnp.where(ids == lanes + index * block, loss_scale * hard_weight, 0.0)
        grad[:, at] = (student - mapped * target_gain - hits).astype(grad.dtype)
        return carry

    lax.fori_loop(0, blocks, finish, 0)

    pieces, span = sent.shape[1] // out.shape[0], sent.shape[2]
    rows = out.shape[0]
    for piece in range(pieces):
        product = lax.dot_general(
            grad[...], whole[piece * span:(piece + 1) * span, :],
            (((1,), (1,)), ((), ())), preferred_element_type=jnp.float32,
        )
        for owner in range(count):
            partial[owner, piece * rows:(piece + 1) * rows, :] = product[owner * rows:(owner + 1) * rows, :]

    def narrow(owner, carry):
        sent[owner] = partial[owner].astype(sent.dtype)
        return carry

    lax.fori_loop(0, count, narrow, 0)

    def share_grad(hop):
        return pltpu.make_async_remote_copy(
            src_ref=sent.at[(me + hop) % count], dst_ref=landed.at[hop],
            send_sem=grad_send.at[hop], recv_sem=grad_recv.at[hop],
            device_id=peer(hop), device_id_type=MESH,
        )

    every(lambda hop: share_grad(hop).start())
    every(lambda hop: share_grad(hop).wait())

    total = lax.fori_loop(
        1, count, lambda hop, total: total + landed[hop].astype(jnp.float32), partial[me]
    )
    for piece in range(pieces):
        out[:, piece * span:(piece + 1) * span] = total[
            piece * rows:(piece + 1) * rows, :
        ].astype(out.dtype)

    for target in range(chips):
        to_core(target).wait_send()
        if target > 0:
            @pl.when(chip < target)
            def _():
                up(target).wait_send()
        if target < last:
            @pl.when(chip > target)
            def _():
                down(target).wait_send()


def student_call(chips, vocabs, dense, peak_row, all_s, all_id, head):
    places, blocks, tokens, block = dense.shape
    count = places * vocabs
    depth, cols = head.shape
    rows = tokens // count
    span = 512
    tall = rows * depth // span
    vmem = pl.BlockSpec(memory_space=pltpu.VMEM)
    dma = pltpu.SemaphoreType.DMA
    return pl.pallas_call(
        functools.partial(student_kernel, chips, vocabs),
        out_shape=jax.ShapeDtypeStruct((rows, depth), jnp.bfloat16),
        in_specs=[vmem, vmem, vmem, vmem, pl.BlockSpec(memory_space=pl.ANY)],
        out_specs=vmem,
        scratch_shapes=[
            pltpu.VMEM((depth, cols), head.dtype),
            pltpu.VMEM((chips, blocks, tokens, block), jnp.bfloat16),
            pltpu.VMEM((chips, blocks, tokens, block), jnp.bfloat16),
            pltpu.VMEM((chips, blocks, tokens, block), jnp.bfloat16),
            pltpu.VMEM((count, 8, tokens), jnp.float32),
            pltpu.VMEM((count, 8, tokens), jnp.float32),
            pltpu.VMEM((tokens, cols), jnp.float32),
            pltpu.VMEM((tokens, cols), jnp.bfloat16),
            pltpu.VMEM((count, tall, span), jnp.float32),
            pltpu.VMEM((count, tall, span), jnp.bfloat16),
            pltpu.VMEM((count, tall, span), jnp.bfloat16),
            dma((cols // chunk_of(cols),)),
            dma((count,)), dma((count,)), dma((count,)), dma((count,)),
            dma((chips,)), dma((chips,)), dma((chips,)), dma((chips,)),
            dma((chips,)), dma((chips,)),
            dma((count,)), dma((count,)),
        ],
        compiler_params=pltpu.CompilerParams(
            collective_id=1, has_side_effects=True, vmem_limit_bytes=vmem_bytes
        ),
    )(dense, peak_row, all_s, all_id, head)


def on_device(
    teacher_hidden, teacher_head, map_dest, map_slot, map_weight,
    student_hidden, student_head, targets,
):
    places = lax.axis_size("dp")
    vocabs = lax.axis_size("vocab")
    chips = places // 2
    block = map_weight.shape[2]
    teacher_blocks, fan = map_dest.shape
    blocks = student_head.shape[1] // block
    wide_ids = jnp.broadcast_to(targets[:, None], (targets.shape[0], block))
    logits, all_s, all_id = teacher_call(chips, teacher_hidden, student_hidden, wide_ids, teacher_head)
    tokens = logits.shape[0]
    peak = jnp.max(logits, axis=1)
    weights = jnp.exp(logits - peak[:, None]).astype(jnp.bfloat16)
    terms = jnp.einsum(
        "gkc,krcd->krgd", weights.reshape(tokens, teacher_blocks, block), map_weight,
        preferred_element_type=jnp.float32,
    ).astype(jnp.bfloat16)
    items = teacher_blocks * fan
    goal = (map_dest * blocks + map_slot).reshape(items)
    marks = (jnp.arange(places * blocks, dtype=jnp.int32)[:, None] == goal[None, :]).astype(jnp.bfloat16)
    dense = jnp.dot(
        marks, terms.reshape(items, tokens * block), preferred_element_type=jnp.float32
    ).astype(jnp.bfloat16).reshape(places, blocks, tokens, block)
    peak_row = jnp.broadcast_to(peak[None, :], (8, tokens))
    return student_call(chips, vocabs, dense, peak_row, all_s, all_id, student_head)


def solution(mesh):
    placed = (
        P(("groups", "dp"), None),
        P(None, ("dp", "vocab")),
        P(("dp", "vocab"), None),
        P(("dp", "vocab"), None),
        P(("dp", "vocab"), None, None, None),
        P(("groups", "dp"), None),
        P(None, ("dp", "vocab")),
        P(("groups", "dp")),
    )
    return jax.shard_map(
        on_device,
        mesh=mesh,
        in_specs=placed,
        out_specs=P(("groups", "dp", "vocab"), None),
        check_vma=False,
    )
```

time: 324 us -> 137 us (0.42)
  blocking collectives: 239 us -> 0 us
  Pallas kernels: 0 us -> 118 us
  matrix products: 63.2 us -> 6.32 us
  starting transfers between devices: 10.9 us -> 0 us
    unnamed x2 -> x0, blocking collectives: 145 us -> none
    pallas_call x0 -> x2, Pallas kernels: none -> 118 us  [the longest x1 90.9 us: student_call(): pl.pallas_call(functools.partial(student_kernel, chips, vocabs), out_shap...]
    dot_general x7 -> x2, matrix products: 63.2 us -> 6.32 us  [the longest x1 3.82 us: on_device(): jnp.einsum('gkc,krcd->krgd', weights.reshape(tokens, teacher_blocks, bloc...]
    pmax x1 -> x0, blocking collectives: 34.2 us -> none  [on_device(): teacher_peak = lax.pmax(jnp.max(teacher_logits, axis=1), ('dp', 'vocab'))]
    all_gather x2 -> x0, blocking collectives: 31 us -> none  [the longest x1 15.8 us: on_device(): lax.all_gather(teacher_hidden, 'dp', axis=0, tiled=True)]
    psum x1 -> x0, blocking collectives: 29.5 us -> none  [on_device(): target_total = lax.psum(jnp.sum(mapped, axis=1), ('dp', 'vocab'))]
    all_to_all x2 -> x0, starting transfers between devices: 10.9 us -> none  [the longest x1 6.33 us: on_device(): lax.all_to_all(slot_marks, 'dp', split_axis=0, concat_axis=0, tiled=True)]
    unnamed x16 -> x7, local copies, waits for them, and re-layouts: 6.49 us -> 4.65 us
  transfers between devices with their start and end apart: 2 -> 0, of which waited for: 0 -> 0; matrix products, arithmetic and copies ran while one was open for 15% -> 0% of each run, Pallas kernels for 0% -> 0%
where the time goes in v1:
time: 137 us; the launch traced here: 135 us
  Pallas kernels  118 us (86%)
  local copies, waits for them, and re-layouts  6.75 us (5%)
  matrix products  6.32 us (5%)
  other arithmetic  3.28 us (2%)
    pallas_call x1, Pallas kernels, student_call(): pl.pallas_call(functools.partial(student_kernel, chips, vocabs), out_shap...  90.9 us
    pallas_call x1, Pallas kernels, teacher_call(): pl.pallas_call(functools.partial(teacher_kernel, chips), out_shape=(jax.S...  27.4 us
    unnamed x7, local copies, waits for them, and re-layouts  4.65 us
    dot_general x1, matrix products, on_device(): jnp.einsum('gkc,krcd->krgd', weights.reshape(tokens, teacher_blocks, bloc...  3.82 us

profile of v1, /device:TPU:0, one launch (start us, length us, event | category | flops | bytes accessed | tf_op | source)
XLA Modules:
  0.0 134.8 jit_solution(12549383265338307315)
XLA Ops:
  0.0 1.3 broadcast_in_dim.4.own_id
  1.3 27.4 %shard_map.82 = (f32[64,6144]{1,0:T(8,128)}, bf16[8,8,4096]{2,1,0:T(8,128)(2,1)}, s32[8,8,128]{2,1,0:T(8,128)}) custom-call(bf16[8,5120]{1,0:T(8,128)(2,1)} %own_t.1, bf16[8,4096]{1,0:T(8,128)(2,1)} %own_s.1, s32[8,128]{1,0:T(8,128)} %broadcast_in_dim.4.own_id, bf16[5120,6144]{1,0:T(8,128)(2,1)} %head.2), custom_call_target="tpu_custom_call" | custom-call | tf_op jit(solution)/shard_map/pallas_call | solution.py:129
  28.8 1.6 %reduce_max.9 = f32[64]{0:T(128)S(1)} reduce(f32[64,6144]{1,0:T(8,128)} %get-tuple-element.8, f32[]{:T(128)} %constant.1.clone.1), dimensions={1}, to_apply=%region_0.0 | reduce | flops 393152 | bytes 1573124 | tf_op jit(solution)/shard_map/reduce_max | solution.py:452
  30.3 1.7 %fusion.5 = bf16[8,8,48,128]{3,1,2,0:T(8,128)(2,1)S(1)} fusion(f32[64,6144]{1,0:T(8,128)} %get-tuple-element.8, f32[64]{0:T(128)S(1)} %reduce_max.9), kind=kLoop, calls=%fused_computation.6 | loop fusion | flops 786432 | bytes 2359552
  32.0 0.1 copy.15
  32.2 0.0 copy-start
  32.2 0.0 copy-start.1
  32.2 3.8 %convolution_convert_fusion.1 = bf16[48,64,4,128]{3,1,2,0:T(8,128)(2,1)S(1)} fusion(bf16[48,4,128,128]{3,2,1,0:T(8,128)(2,1)} %param.12, bf16[64,48,128,1]{2,1,0,3:T(8,128)(2,1)S(1)} %bitcast.20), kind=kOutput, calls=%fused_computation.3 | convolution fusion | flops 404226048 | bytes 10223616 | tf_op jit(solution)/shard_map/gkc,krcd->krgd/dot_general | solution.py:454
  36.0 0.0 copy-done
  36.0 0.0 copy-done.1
  36.0 0.1 copy.10
  36.1 0.1 eq.16
  36.2 2.5 %fusion.2 = bf16[32,8,64,128]{3,1,2,0:T(8,128)(2,1)S(1)} fusion(bf16[24,8,64,128]{3,2,1,0:T(8,128)(2,1)S(1)} %bitcast.19, s32[192]{0:T(256)S(1)} %eq.16), kind=kOutput, calls=%fused_computation.4 | convolution fusion | flops 807452672 | bytes 7340800 | tf_op jit(solution)/shard_map/dot_general | solution.py:461
  38.7 3.1 %copy.17 = bf16[32,8,64,128]{3,2,1,0:T(8,128)(2,1)} copy(bf16[32,8,64,128]{3,1,2,0:T(8,128)(2,1)S(1)} %fusion.2) | data formatting | bytes 8388608
  41.9 0.6 broadcast_in_dim.5.peak_row
  42.5 90.9 %shard_map.83 = bf16[4,4096]{1,0:T(4,128)(2,1)} custom-call(bf16[8,32,64,128]{3,2,1,0:T(8,128)(2,1)} %bitcast.18, f32[8,64]{1,0:T(8,128)} %broadcast_in_dim.5.peak_row, bf16[8,8,4096]{2,1,0:T(8,128)(2,1)} %get-tuple-element.9.all_s, s32[8,8,128]{2,1,0:T(8,128)} %get-tuple-element.10.all_id, bf16[4096,4096]{1,0:T(8,128)(2,1)} %head.3), custom_call_target="tpu_custom_call" | custom-call | tf_op jit(solution)/shard_map/pallas_call | solution.py:410
  133.4 1.4 %copy.27 = bf16[4,4096]{1,0:T(4,128)(2,1)} copy(bf16[4,4096]{1,0:T(4,128)(2,1)} %shard_map.83) | data formatting | bytes 65536
  (1 shorter events, 0.0 us)
Async XLA Ops:
  32.2 3.9 %copy-start = (s32[48,4]{0,1:T(4,128)S(1)}, s32[48,4]{0,1:T(4,128)}, u32[]{:S(2)}) copy-start(s32[48,4]{0,1:T(4,128)} %param.11) | copy-start | bytes 2308
  32.2 3.8 %copy-start.1 = (s32[48,4]{0,1:T(4,128)S(1)}, s32[48,4]{0,1:T(4,128)}, u32[]{:S(2)}) copy-start(s32[48,4]{0,1:T(4,128)} %param.10) | copy-start | bytes 2308

commit v2 on v1

v2 whole, which is shorter than its diff:
```python
import functools

import jax
import jax.numpy as jnp
from jax import lax
from jax.experimental import pallas as pl
from jax.experimental.pallas import tpu as pltpu
from jax.sharding import PartitionSpec as P

MESH = pl.DeviceIdType.MESH
hard_weight = 0.25
loss_scale = 64.0
vmem_bytes = 60 * 1024 * 1024


def chunk_of(cols):
    for size in (512, 256, 128):
        if cols % size == 0:
            return size
    return cols


def teacher_kernel(
    chips, own_t, own_s, own_id, head, logits, all_s, all_id, peak_row,
    held_t, held_s, held_id, tiles, tile_sem, send_sem, recv_sem, pass_sem, land_sem,
):
    place = lax.axis_index("dp")
    chip, core = place // 2, place % 2
    slots, width = tiles.shape[0], tiles.shape[2]
    steps = head.shape[1] // width

    def fetch(step, slot):
        return pltpu.make_async_copy(
            head.at[:, pl.ds(pl.multiple_of(step * width, width), width)],
            tiles.at[slot],
            tile_sem.at[slot],
        )

    for slot in range(min(slots, steps)):
        fetch(slot, slot).start()
    held_t[place] = own_t[...]
    held_s[place] = own_s[...]
    rows = own_t.shape[0]
    same = lax.broadcasted_iota(jnp.int32, (rows, rows), 0) == lax.broadcasted_iota(
        jnp.int32, (rows, rows), 1
    )
    held_id[place] = jnp.broadcast_to(
        jnp.sum(jnp.where(same, own_id[...], 0), axis=1, keepdims=True), held_id.shape[1:]
    )

    barrier = pltpu.get_barrier_semaphore()
    partner = chip * 2 + (1 - core)
    for hop in range(1, chips):
        other = (chip + hop) % chips * 2 + core
        pl.semaphore_signal(barrier, inc=1, device_id={"dp": other}, device_id_type=MESH)
    pl.semaphore_signal(barrier, inc=1, device_id={"dp": partner}, device_id_type=MESH)
    pl.semaphore_wait(barrier, chips)

    helds = (held_t, held_id, held_s)

    def across(kind, hop):
        return pltpu.make_async_remote_copy(
            src_ref=helds[kind].at[place],
            dst_ref=helds[kind].at[place],
            send_sem=send_sem.at[kind, hop],
            recv_sem=recv_sem.at[kind, hop],
            device_id={"dp": (chip + hop) % chips * 2 + core},
            device_id_type=MESH,
        )

    def between(kind, hop):
        block = (chip + chips - hop) % chips * 2 + core
        return pltpu.make_async_remote_copy(
            src_ref=helds[kind].at[block],
            dst_ref=helds[kind].at[block],
            send_sem=pass_sem.at[kind, hop],
            recv_sem=land_sem.at[kind, hop],
            device_id={"dp": partner},
            device_id_type=MESH,
        )

    for kind in range(3):
        for hop in range(1, chips):
            across(kind, hop).start()
        between(kind, 0).start()
    for hop in range(1, chips):
        across(0, hop).wait_recv()
        between(0, hop).start()
    for hop in range(chips):
        between(0, hop).wait_recv()

    tokens = held_t.shape[0] * held_t.shape[1]

    def multiply(step, carry):
        slot = step % slots
        fetch(step, slot).wait()
        value = jnp.dot(
            held_t[...].reshape(tokens, held_t.shape[2]),
            tiles[slot],
            preferred_element_type=jnp.float32,
        )
        logits[:, pl.ds(pl.multiple_of(step * width, width), width)] = value
        for start in range(0, width, 128):
            carry = jnp.maximum(carry, value[:, start:start + 128])

        @pl.when(step + slots < steps)
        def _():
            fetch(step + slots, slot).start()

        return carry

    middle = steps // 2
    highest = jnp.full((tokens, 128), -jnp.inf, jnp.float32)
    highest = lax.fori_loop(0, middle, multiply, highest)
    for kind in (1, 2):
        for hop in range(1, chips):
            across(kind, hop).wait_recv()
            between(kind, hop).start()
    highest = lax.fori_loop(middle, steps, multiply, highest)
    for kind in (1, 2):
        for hop in range(chips):
            between(kind, hop).wait_recv()
    for kind in range(3):
        for hop in range(1, chips):
            across(kind, hop).wait_send()
        for hop in range(chips):
            between(kind, hop).wait_send()
    all_s[...] = held_s[...]
    all_id[...] = held_id[...]
    diagonal = lax.broadcasted_iota(jnp.int32, (tokens, tokens), 0) == lax.broadcasted_iota(
        jnp.int32, (tokens, tokens), 1
    )
    peak = jnp.max(highest, axis=1, keepdims=True)
    peak_row[...] = jnp.broadcast_to(
        jnp.sum(jnp.where(diagonal, peak, 0.0), axis=0, keepdims=True), peak_row.shape
    )


def teacher_call(chips, own_t, own_s, own_id, head):
    depth, cols = head.shape
    width = chunk_of(cols)
    slots = min(8, cols // width)
    places = chips * 2
    rows = own_t.shape[0]
    vmem = pl.BlockSpec(memory_space=pltpu.VMEM)
    return pl.pallas_call(
        functools.partial(teacher_kernel, chips),
        out_shape=(
            jax.ShapeDtypeStruct((places * rows, cols), jnp.float32),
            jax.ShapeDtypeStruct((places,) + own_s.shape, own_s.dtype),
            jax.ShapeDtypeStruct((places, rows, 128), own_id.dtype),
            jax.ShapeDtypeStruct((8, places * rows), jnp.float32),
        ),
        in_specs=[vmem, vmem, vmem, pl.BlockSpec(memory_space=pl.ANY)],
        out_specs=(vmem, vmem, vmem, vmem),
        scratch_shapes=[
            pltpu.VMEM((places,) + own_t.shape, own_t.dtype),
            pltpu.VMEM((places,) + own_s.shape, own_s.dtype),
            pltpu.VMEM((places, rows, 128), own_id.dtype),
            pltpu.VMEM((slots, depth, width), head.dtype),
            pltpu.SemaphoreType.DMA((slots,)),
            pltpu.SemaphoreType.DMA((3, chips)),
            pltpu.SemaphoreType.DMA((3, chips)),
            pltpu.SemaphoreType.DMA((3, chips)),
            pltpu.SemaphoreType.DMA((3, chips)),
        ],
        compiler_params=pltpu.CompilerParams(
            collective_id=0, has_side_effects=True, vmem_limit_bytes=vmem_bytes
        ),
    )(own_t, own_s, own_id, head)


def student_kernel(
    chips, vocabs, dense, peak_row, all_s, all_id, head, out,
    whole, summed, up_in, down_in, peaks, stats, logits, grad, product, partial, sent, given, landed,
    tile_sem, peak_send, peak_recv, stat_send, stat_recv, core_send, core_recv,
    up_send, up_recv, down_send, down_recv, give_send, give_recv, grad_send, grad_recv,
):
    place, vocab = lax.axis_index("dp"), lax.axis_index("vocab")
    chip, core = place // 2, place % 2
    partner = chip * 2 + (1 - core)
    count = chips * 2 * vocabs
    me = place * vocabs + vocab
    blocks, tokens, block = summed.shape[1:]
    depth, cols = head.shape
    width = chunk_of(cols)
    steps = cols // width
    last = chips - 1
    parts = core_send.shape[0]
    share_of = blocks // parts

    def fetch(step):
        at = pl.ds(pl.multiple_of(step * width, width), width)
        return pltpu.make_async_copy(head.at[:, at], whole.at[:, at], tile_sem.at[step])

    for step in range(steps):
        fetch(step).start()
    peaks[me] = peak_row[...]

    def every(body):
        lax.fori_loop(1, count, lambda hop, carry: (body(hop), carry)[1], 0)

    def peer(hop):
        other = (me + hop) % count
        return {"dp": other // vocabs, "vocab": other % vocabs}

    barrier = pltpu.get_barrier_semaphore()
    every(lambda hop: pl.semaphore_signal(barrier, inc=1, device_id=peer(hop), device_id_type=MESH))
    pl.semaphore_wait(barrier, count - 1)

    def share(ref, send_sem, recv_sem):
        def one(hop):
            return pltpu.make_async_remote_copy(
                src_ref=ref.at[me], dst_ref=ref.at[me],
                send_sem=send_sem.at[hop], recv_sem=recv_sem.at[hop],
                device_id=peer(hop), device_id_type=MESH,
            )
        return one

    share_peak = share(peaks, peak_send, peak_recv)
    share_stat = share(stats, stat_send, stat_recv)
    every(lambda hop: share_peak(hop).start())

    order = []
    for near in range((chips + 1) // 2):
        order += [last - near] + ([near] if near != last - near else [])

    def to_core(part, target):
        return pltpu.make_async_remote_copy(
            src_ref=dense.at[target * 2 + 1 - core, pl.ds(part * share_of, share_of)],
            dst_ref=summed.at[target, pl.ds(part * share_of, share_of)],
            send_sem=core_send.at[part, target], recv_sem=core_recv.at[part, target],
            device_id={"dp": partner}, device_id_type=MESH,
        )

    def up(part, target):
        return pltpu.make_async_remote_copy(
            src_ref=summed.at[target, pl.ds(part * share_of, share_of)],
            dst_ref=up_in.at[target, pl.ds(part * share_of, share_of)],
            send_sem=up_send.at[part, target], recv_sem=up_recv.at[part, target],
            device_id={"dp": (chip + 1) % chips * 2 + core}, device_id_type=MESH,
        )

    def down(part, target):
        return pltpu.make_async_remote_copy(
            src_ref=summed.at[target, pl.ds(part * share_of, share_of)],
            dst_ref=down_in.at[target, pl.ds(part * share_of, share_of)],
            send_sem=down_send.at[part, target], recv_sem=down_recv.at[part, target],
            device_id={"dp": (chip + last) % chips * 2 + core}, device_id_type=MESH,
        )

    for part in range(parts):
        for target in order:
            to_core(part, target).start()

    eye = lax.broadcasted_iota(jnp.int32, (tokens, tokens), 0) == lax.broadcasted_iota(
        jnp.int32, (tokens, tokens), 1
    )

    def column(row):
        return jnp.sum(jnp.where(eye, row, 0.0), axis=1, keepdims=True)

    def row_of(col):
        return jnp.sum(jnp.where(eye, col, 0.0), axis=0, keepdims=True)

    def add_rows(index, total):
        tile = dense[index // blocks, index % blocks]
        return total + tile.astype(jnp.float32)

    row_total = lax.fori_loop(
        0, 2 * chips * blocks, add_rows, jnp.zeros((tokens, block), jnp.float32)
    )
    every(lambda hop: share_peak(hop).wait())
    peak = column(jnp.max(peaks[:, 0:1, :], axis=0))
    own_scale = jnp.exp(column(peaks[me, 0:1, :]) - peak)
    partner_scale = jnp.exp(column(peaks[partner * vocabs + vocab, 0:1, :]) - peak)
    term_total = own_scale * jnp.sum(row_total, axis=1, keepdims=True)
    own_wide = jnp.broadcast_to(own_scale, (tokens, block))
    partner_wide = jnp.broadcast_to(partner_scale, (tokens, block))

    def combine(part):
        for target in order:
            to_core(part, target).wait_recv()

            def one(index, carry):
                summed[target, index] = (
                    dense[target * 2 + core, index].astype(jnp.float32) * own_wide
                    + summed[target, index].astype(jnp.float32) * partner_wide
                ).astype(summed.dtype)
                return carry

            lax.fori_loop(part * share_of, (part + 1) * share_of, one, 0)

    def multiply(step, carry):
        fetch(step).wait()
        at = pl.ds(pl.multiple_of(step * width, width), width)
        logits[:, at] = jnp.dot(
            all_s[...].reshape(tokens, depth), whole[:, at], preferred_element_type=jnp.float32
        )
        return carry

    def add_in(part, target, ref):
        def one(index, carry):
            summed[target, index] = (
                summed[target, index].astype(jnp.float32) + ref[target, index].astype(jnp.float32)
            ).astype(summed.dtype)
            return carry

        lax.fori_loop(part * share_of, (part + 1) * share_of, one, 0)

    turns = [(part, turn) for part in range(parts) for turn in range(last)]

    def hop_up(at):
        part, high = turns[at][0], last - turns[at][1]

        @pl.when(chip == 0)
        def _():
            if at >= 2:
                up(turns[at - 2][0], last - turns[at - 2][1]).wait_send()
            up(part, high).start()

        if high > 1:
            @pl.when((chip > 0) & (chip < high))
            def _():
                up(part, high).wait_recv()
                add_in(part, high, up_in)
                up(part, high).start()

    def hop_down(at):
        part, low = turns[at]

        @pl.when(chip == last)
        def _():
            if at >= 2:
                down(*turns[at - 2]).wait_send()
            down(part, low).start()

        if low < last - 1:
            @pl.when((chip < last) & (chip > low))
            def _():
                down(part, low).wait_recv()
                add_in(part, low, down_in)
                down(part, low).start()

    def hop(at):
        pl.when(chip * 2 < chips)(lambda: hop_up(at))
        hop_down(at)
        pl.when(chip * 2 >= chips)(lambda: hop_up(at))

    ids = all_id[...].reshape(tokens, block)
    lanes = lax.broadcasted_iota(jnp.int32, (tokens, block), 1) + me * cols

    def totals():
        target_total = column(jnp.sum(stats[:, 0:1, :], axis=0))
        peak_all = jnp.max(stats[:, 1:2, :], axis=0)
        student_total = column(
            jnp.sum(stats[:, 2:3, :] * jnp.exp(stats[:, 1:2, :] - peak_all), axis=0)
        )
        return tuple(
            jnp.broadcast_to(value, (tokens, block))
            for value in (
                column(peak_all),
                loss_scale / student_total,
                loss_scale * (1.0 - hard_weight) / target_total,
            )
        )

    halves = partial.shape[0]
    rows, span = out.shape[0], partial.shape[3]
    pieces = depth // span
    per_half = pieces // halves

    def finish(part, wide):
        peak_wide, student_gain, target_gain = wide
        for target in range(chips):
            if target > 0:
                @pl.when(chip == target)
                def _():
                    up(part, target).wait_recv()
            if target < last:
                @pl.when(chip == target)
                def _():
                    down(part, target).wait_recv()

        def one(index, carry):
            mapped = summed[chip, index].astype(jnp.float32)
            mapped = mapped + jnp.where(chip > 0, up_in[chip, index].astype(jnp.float32), 0.0)
            mapped = mapped + jnp.where(chip < last, down_in[chip, index].astype(jnp.float32), 0.0)
            at = pl.ds(pl.multiple_of(index * block, block), block)
            student = jnp.exp(logits[:, at] - peak_wide) * student_gain
            hits = jnp.where(ids == lanes + index * block, loss_scale * hard_weight, 0.0)
            grad[:, at] = (student - mapped * target_gain - hits).astype(grad.dtype)
            return carry

        lax.fori_loop(part * share_of, (part + 1) * share_of, one, 0)

    def piece_of(part, piece):
        across = slice(part * share_of * block, (part + 1) * share_of * block)
        return lax.dot_general(
            grad[:, across], whole[piece * span:(piece + 1) * span, across],
            (((1,), (1,)), ((), ())), preferred_element_type=jnp.float32,
        )

    def accumulate(part):
        for piece in range(pieces):
            at = slice(piece * span, (piece + 1) * span)
            value = piece_of(part, piece)
            product[:, at] = value if part == 0 else product[:, at] + value

    def give(half, target):
        return pltpu.make_async_remote_copy(
            src_ref=sent.at[half, pl.ds((target * 2 + 1 - core) * vocabs, vocabs)],
            dst_ref=given.at[half, target],
            send_sem=give_send.at[half, target], recv_sem=give_recv.at[half, target],
            device_id={"dp": partner}, device_id_type=MESH,
        )

    column_me = chip * vocabs + vocab
    column_count = chips * vocabs

    def owner_of(step):
        other = (column_me + step) % column_count
        return other // vocabs, other % vocabs

    def share_grad(half, step):
        target, side = owner_of(step)
        return pltpu.make_async_remote_copy(
            src_ref=sent.at[half, (target * 2 + core) * vocabs + side], dst_ref=landed.at[half, step],
            send_sem=grad_send.at[half, step], recv_sem=grad_recv.at[half, step],
            device_id={"dp": target * 2 + core, "vocab": side}, device_id_type=MESH,
        )

    combine(0)
    busy = max(1, (len(turns) + 1) // 2)
    done = 0
    wide = None
    accumulated = 0
    for at, (part, turn) in enumerate(turns):
        hop(at)
        if at < busy:
            until = steps * (at + 1) // busy
            lax.fori_loop(done, until, multiply, 0)
            done = until
        if at == busy - 1:
            own_peak = jnp.max(logits[...], axis=1, keepdims=True)
            own_sum = jnp.sum(jnp.exp(logits[...] - own_peak), axis=1, keepdims=True)
            stats[me, 0:1, :] = row_of(term_total)
            stats[me, 1:2, :] = row_of(own_peak)
            stats[me, 2:3, :] = row_of(own_sum)
            stats[me, 3:8, :] = jnp.zeros((5, tokens), jnp.float32)
            every(lambda step: share_stat(step).start())
        if turn == last - 1 and part + 1 < parts:
            combine(part + 1)
        if at >= busy + last - 1 and at < len(turns) - 1 and accumulated < part:
            if wide is None:
                every(lambda step: share_stat(step).wait())
                wide = totals()
            finish(accumulated, wide)
            accumulate(accumulated)
            accumulated += 1
    if wide is None:
        every(lambda step: share_stat(step).wait())
        wide = totals()
    for part in range(accumulated, parts - 1):
        finish(part, wide)
        accumulate(part)
    finish(parts - 1, wide)

    for half in range(halves):
        for inner in range(per_half):
            piece = half * per_half + inner
            value = piece_of(parts - 1, piece)
            if parts > 1:
                value = value + product[:, piece * span:(piece + 1) * span]
            for owner in range(count):
                partial[half, owner, inner * rows:(inner + 1) * rows, :] = value[owner * rows:(owner + 1) * rows, :]
        for target in range(chips):
            first = (target * 2 + 1 - core) * vocabs
            for side in range(vocabs):
                sent[half, first + side] = partial[half, first + side].astype(sent.dtype)
            give(half, target).start()

    for half in range(halves):
        for target in range(chips):
            give(half, target).wait_recv()

        def pass_on(step, carry):
            target, side = owner_of(step)
            owner = (target * 2 + core) * vocabs + side
            sent[half, owner] = (
                partial[half, owner] + given[half, target, side].astype(jnp.float32)
            ).astype(sent.dtype)
            share_grad(half, step).start()
            return carry

        lax.fori_loop(1, column_count, pass_on, 0)

    for half in range(halves):
        def arrive(step, total):
            share_grad(half, step).wait_recv()
            return total + landed[half, step].astype(jnp.float32)

        total = lax.fori_loop(
            1, column_count, arrive, partial[half, me] + given[half, chip, vocab].astype(jnp.float32)
        )
        for inner in range(per_half):
            piece = half * per_half + inner
            out[:, piece * span:(piece + 1) * span] = total[
                inner * rows:(inner + 1) * rows, :
            ].astype(out.dtype)

    for half in range(halves):
        for target in range(chips):
            give(half, target).wait_send()
        lax.fori_loop(1, column_count, lambda step, carry: (share_grad(half, step).wait_send(), carry)[1], 0)
    for at, (part, turn) in enumerate(turns):
        high, low = last - turn, turn
        late = at >= len(turns) - 2

        @pl.when((chip < high) if late else ((chip > 0) & (chip < high)))
        def _():
            up(part, high).wait_send()

        @pl.when((chip > low) if late else ((chip < last) & (chip > low)))
        def _():
            down(part, low).wait_send()
    for part in range(parts):
        for target in range(chips):
            to_core(part, target).wait_send()


def student_call(chips, vocabs, dense, peak_row, all_s, all_id, head):
    places, blocks, tokens, block = dense.shape
    count = places * vocabs
    depth, cols = head.shape
    rows = tokens // count
    span = 512
    tall = rows * depth // span
    halves = 2 if tall % 32 == 0 else 1
    tall = tall // halves
    parts = 4 if blocks % 32 == 0 else 1
    vmem = pl.BlockSpec(memory_space=pltpu.VMEM)
    dma = pltpu.SemaphoreType.DMA
    return pl.pallas_call(
        functools.partial(student_kernel, chips, vocabs),
        out_shape=jax.ShapeDtypeStruct((rows, depth), jnp.bfloat16),
        in_specs=[vmem, vmem, vmem, vmem, pl.BlockSpec(memory_space=pl.ANY)],
        out_specs=vmem,
        scratch_shapes=[
            pltpu.VMEM((depth, cols), head.dtype),
            pltpu.VMEM((chips, blocks, tokens, block), jnp.bfloat16),
            pltpu.VMEM((chips, blocks, tokens, block), jnp.bfloat16),
            pltpu.VMEM((chips, blocks, tokens, block), jnp.bfloat16),
            pltpu.VMEM((count, 8, tokens), jnp.float32),
            pltpu.VMEM((count, 8, tokens), jnp.float32),
            pltpu.VMEM((tokens, cols), jnp.float32),
            pltpu.VMEM((tokens, cols), jnp.bfloat16),
            pltpu.VMEM((tokens, depth), jnp.float32),
            pltpu.VMEM((halves, count, tall, span), jnp.float32),
            pltpu.VMEM((halves, count, tall, span), jnp.bfloat16),
            pltpu.VMEM((halves, chips, vocabs, tall, span), jnp.bfloat16),
            pltpu.VMEM((halves, chips * vocabs, tall, span), jnp.bfloat16),
            dma((cols // chunk_of(cols),)),
            dma((count,)), dma((count,)), dma((count,)), dma((count,)),
            dma((parts, chips)), dma((parts, chips)), dma((parts, chips)),
            dma((parts, chips)), dma((parts, chips)), dma((parts, chips)),
            dma((halves, chips)), dma((halves, chips)),
            dma((halves, chips * vocabs)), dma((halves, chips * vocabs)),
        ],
        compiler_params=pltpu.CompilerParams(
            collective_id=1, has_side_effects=True, vmem_limit_bytes=vmem_bytes
        ),
    )(dense, peak_row, all_s, all_id, head)


def on_device(
    teacher_hidden, teacher_head, map_dest, map_slot, map_weight,
    student_hidden, student_head, targets,
):
    places = lax.axis_size("dp")
    vocabs = lax.axis_size("vocab")
    chips = places // 2
    block = map_weight.shape[2]
    teacher_blocks, fan = map_dest.shape
    blocks = student_head.shape[1] // block
    logits, all_s, all_id, peak_row = teacher_call(
        chips, teacher_hidden, student_hidden, targets[None, :], teacher_head
    )
    tokens = logits.shape[0]
    weights = jnp.exp(logits - peak_row[0][:, None]).astype(jnp.bfloat16)
    terms = jnp.einsum(
        "gkc,krcd->krgd", weights.reshape(tokens, teacher_blocks, block), map_weight,
        preferred_element_type=jnp.float32,
    ).astype(jnp.bfloat16)
    items = teacher_blocks * fan
    goal = (map_dest * blocks + map_slot).reshape(items)
    marks = (jnp.arange(places * blocks, dtype=jnp.int32)[:, None] == goal[None, :]).astype(jnp.bfloat16)
    dense = jnp.dot(
        marks, terms.reshape(items, tokens * block), preferred_element_type=jnp.float32
    ).astype(jnp.bfloat16).reshape(places, blocks, tokens, block)
    return student_call(chips, vocabs, dense, peak_row, all_s, all_id, student_head)


def solution(mesh):
    placed = (
        P(("groups", "dp"), None),
        P(None, ("dp", "vocab")),
        P(("dp", "vocab"), None),
        P(("dp", "vocab"), None),
        P(("dp", "vocab"), None, None, None),
        P(("groups", "dp"), None),
        P(None, ("dp", "vocab")),
        P(("groups", "dp")),
    )
    return jax.shard_map(
        on_device,
        mesh=mesh,
        in_specs=placed,
        out_specs=P(("groups", "dp", "vocab"), None),
        check_vma=False,
    )
```

time: 137 us -> 114 us (0.83); the launches traced: 135 us -> 113 us
  Pallas kernels: 118 us -> 99.1 us
    pallas_call x1, Pallas kernels: 90.9 us -> 71.5 us  [student_call(): pl.pallas_call(functools.partial(student_kernel, chips, vocabs), out_shap...]
    broadcast_in_dim x2 -> x0, local copies, waits for them, and re-layouts: 1.91 us -> none  [the longest x1 1.31 us: on_device(): wide_ids = jnp.broadcast_to(targets[:, None], (targets.shape[0], block))]
    reduce_max x1 -> x0, other arithmetic: 1.58 us -> none  [on_device(): peak = jnp.max(logits, axis=1)]
    unnamed x7 -> x3, local copies, waits for them, and re-layouts: 4.65 us -> 4.64 us
where the time goes in v2:
time: 114 us; the launch traced here: 113 us
  Pallas kernels  99.1 us (87%)
  matrix products  6.32 us (6%)
  local copies, waits for them, and re-layouts  5.51 us (5%)
  other arithmetic  2.39 us (2%)
    pallas_call x1, Pallas kernels, student_call(): pl.pallas_call(functools.partial(student_kernel, chips, vocabs), out_shap...  71.5 us
    pallas_call x1, Pallas kernels, teacher_call(): pl.pallas_call(functools.partial(teacher_kernel, chips), out_shape=(jax.S...  27.6 us
    unnamed x3, local copies, waits for them, and re-layouts  4.64 us
    dot_general x1, matrix products, on_device(): jnp.einsum('gkc,krcd->krgd', weights.reshape(tokens, teacher_blocks, bloc...  3.81 us
    dot_general x1, matrix products, on_device(): jnp.dot(marks, terms.reshape(items, tokens * block), preferred_element_ty...  2.51 us

profile of v2, /device:TPU:0, one launch (start us, length us, event | category | flops | bytes accessed | tf_op | source)
XLA Modules:
  0.0 113.3 jit_solution(7820137096090410022)
XLA Ops:
  0.0 0.7 multiply_add_fusion
  0.7 0.1 copy.10
  0.8 0.1 eq.16
  0.9 27.6 %shard_map.82 = (f32[64,6144]{1,0:T(8,128)}, bf16[8,8,4096]{2,1,0:T(8,128)(2,1)}, s32[8,8,128]{2,1,0:T(8,128)}, f32[8,64]{1,0:T(8,128)}) custom-call(bf16[8,5120]{1,0:T(8,128)(2,1)} %own_t.1, bf16[8,4096]{1,0:T(8,128)(2,1)} %own_s.1, s32[1,8]{1,0:T(1,128)} %bitcast.24, bf16[5120,6144]{1,0:T(8,128)(2,1)} %head.2), custom_call_target="tpu_custom_call" | custom-call | tf_op jit(solution)/shard_map/pallas_call | solution.py:146
  28.5 0.7 slice_bitcast_fusion
  29.1 1.7 %fusion.5 = bf16[8,8,48,128]{3,1,2,0:T(8,128)(2,1)S(1)} fusion(f32[64,6144]{1,0:T(8,128)} %get-tuple-element.9, f32[64]{0:T(128)S(1)} %slice_bitcast_fusion), kind=kLoop, calls=%fused_computation.6 | loop fusion | flops 786432 | bytes 2359552
  30.8 0.1 copy.15
  31.0 3.8 %convolution_convert_fusion.1 = bf16[48,64,4,128]{3,1,2,0:T(8,128)(2,1)S(1)} fusion(bf16[48,4,128,128]{3,2,1,0:T(8,128)(2,1)} %param.12, bf16[64,48,128,1]{2,1,0,3:T(8,128)(2,1)S(1)} %bitcast.23), kind=kOutput, calls=%fused_computation.3 | convolution fusion | flops 404226048 | bytes 10223616 | tf_op jit(solution)/shard_map/gkc,krcd->krgd/dot_general | solution.py:591
  34.8 2.5 %fusion.2 = bf16[32,8,64,128]{3,1,2,0:T(8,128)(2,1)S(1)} fusion(bf16[24,8,64,128]{3,2,1,0:T(8,128)(2,1)S(1)} %bitcast.22, s32[192]{0:T(256)S(1)} %eq.16), kind=kOutput, calls=%fused_computation.4 | convolution fusion | flops 807452672 | bytes 7340800 | tf_op jit(solution)/shard_map/dot_general | solution.py:598
  37.3 3.1 %copy.17 = bf16[32,8,64,128]{3,2,1,0:T(8,128)(2,1)} copy(bf16[32,8,64,128]{3,1,2,0:T(8,128)(2,1)S(1)} %fusion.2) | data formatting | bytes 8388608
  40.4 71.5 %shard_map.83 = bf16[4,4096]{1,0:T(4,128)(2,1)} custom-call(bf16[8,32,64,128]{3,2,1,0:T(8,128)(2,1)} %bitcast.21, f32[8,64]{1,0:T(8,128)} %get-tuple-element.10.peak_row, bf16[8,8,4096]{2,1,0:T(8,128)(2,1)} %get-tuple-element.11.all_s, s32[8,8,128]{2,1,0:T(8,128)} %get-tuple-element.12.all_id, bf16[4096,4096]{1,0:T(8,128)(2,1)} %head.3), custom_call_target="tpu_custom_call" | custom-call | tf_op jit(solution)/shard_map/pallas_call | solution.py:544
  111.9 1.4 %copy.27 = bf16[4,4096]{1,0:T(4,128)(2,1)} copy(bf16[4,4096]{1,0:T(4,128)(2,1)} %shard_map.83) | data formatting | bytes 65536

commit v3 on v2

--- a/solution.py
+++ b/solution.py
@@ -21,7 +21,7 @@
 
 
 def teacher_kernel(
-    chips, own_t, own_s, own_id, head, logits, all_s, all_id, peak_row,
+    chips, own_t, own_s, own_id, head, logits, all_s, all_id, peak_row, peak_wide,
     held_t, held_s, held_id, tiles, tile_sem, send_sem, recv_sem, pass_sem, land_sem,
 ):
     place = lax.axis_index("dp")
@@ -79,13 +79,16 @@
             device_id_type=MESH,
         )
 
-    for kind in range(3):
+    for kind in range(2):
         for hop in range(1, chips):
             across(kind, hop).start()
         between(kind, 0).start()
     for hop in range(1, chips):
         across(0, hop).wait_recv()
         between(0, hop).start()
+    for hop in range(1, chips):
+        across(2, hop).start()
+    between(2, 0).start()
     for hop in range(chips):
         between(0, hop).wait_recv()
 
@@ -131,6 +134,7 @@
         jnp.int32, (tokens, tokens), 1
     )
     peak = jnp.max(highest, axis=1, keepdims=True)
+    peak_wide[...] = jnp.broadcast_to(peak, peak_wide.shape)
     peak_row[...] = jnp.broadcast_to(
         jnp.sum(jnp.where(diagonal, peak, 0.0), axis=0, keepdims=True), peak_row.shape
     )
@@ -150,9 +154,10 @@
             jax.ShapeDtypeStruct((places,) + own_s.shape, own_s.dtype),
             jax.ShapeDtypeStruct((places, rows, 128), own_id.dtype),
             jax.ShapeDtypeStruct((8, places * rows), jnp.float32),
+            jax.ShapeDtypeStruct((places * rows, 128), jnp.float32),
         ),
         in_specs=[vmem, vmem, vmem, pl.BlockSpec(memory_space=pl.ANY)],
-        out_specs=(vmem, vmem, vmem, vmem),
+        out_specs=(vmem,) * 5,
         scratch_shapes=[
             pltpu.VMEM((places,) + own_t.shape, own_t.dtype),
             pltpu.VMEM((places,) + own_s.shape, own_s.dtype),
@@ -168,6 +173,57 @@
             collective_id=0, has_side_effects=True, vmem_limit_bytes=vmem_bytes
         ),
     )(own_t, own_s, own_id, head)
+
+
+def map_kernel(goal, logits, peak, weight, dense, total):
+    step = pl.program_id(0)
+    group, fan, block = weight.shape[0], weight.shape[1], weight.shape[2]
+
+    @pl.when(step == 0)
+    def _():
+        def clear(index, carry):
+            total[index] = jnp.zeros(total.shape[1:], total.dtype)
+            return carry
+
+        lax.fori_loop(0, total.shape[0], clear, 0, unroll=4)
+
+    for inner in range(group):
+        part = jnp.exp(logits[:, inner * block:(inner + 1) * block] - peak[...]).astype(jnp.bfloat16)
+        terms = [
+            jnp.dot(part, weight[inner, entry], preferred_element_type=jnp.float32).astype(jnp.bfloat16)
+            for entry in range(fan)
+        ]
+        for entry in range(fan):
+            spot = goal[(step * group + inner) * fan + entry]
+            total[spot] += terms[entry].astype(jnp.float32)
+
+    @pl.when(step == pl.num_programs(0) - 1)
+    def _():
+        def narrow(index, carry):
+            dense[index] = total[index].astype(dense.dtype)
+            return carry
+
+        lax.fori_loop(0, total.shape[0], narrow, 0, unroll=4)
+
+
+def map_call(goal, logits, peak, weight, spots):
+    teacher_blocks, fan, block, wide = weight.shape
+    tokens = logits.shape[0]
+    group = 8 if teacher_blocks % 8 == 0 else teacher_blocks
+    return pl.pallas_call(
+        map_kernel,
+        grid=(teacher_blocks // group,),
+        out_shape=jax.ShapeDtypeStruct((spots, tokens, wide), jnp.bfloat16),
+        in_specs=[
+            pl.BlockSpec(memory_space=pltpu.SMEM),
+            pl.BlockSpec((tokens, group * block), lambda step: (0, step)),
+            pl.BlockSpec((tokens, block), lambda step: (0, 0)),
+            pl.BlockSpec((group, fan, block, wide), lambda step: (step, 0, 0, 0)),
+        ],
+        out_specs=pl.BlockSpec((spots, tokens, wide), lambda step: (0, 0, 0)),
+        scratch_shapes=[pltpu.VMEM((spots, tokens, wide), jnp.float32)],
+        compiler_params=pltpu.CompilerParams(vmem_limit_bytes=vmem_bytes),
+    )(goal, logits, peak, weight)
 
 
 def student_kernel(
@@ -249,9 +305,8 @@
             device_id={"dp": (chip + last) % chips * 2 + core}, device_id_type=MESH,
         )
 
-    for part in range(parts):
-        for target in order:
-            to_core(part, target).start()
+    for target in order:
+        to_core(0, target).start()
 
     eye = lax.broadcasted_iota(jnp.int32, (tokens, tokens), 0) == lax.broadcasted_iota(
         jnp.int32, (tokens, tokens), 1
@@ -431,6 +486,9 @@
         )
 
     combine(0)
+    for part in range(1, parts):
+        for target in order:
+            to_core(part, target).start()
     busy = max(1, (len(turns) + 1) // 2)
     done = 0
     wide = None
@@ -583,21 +641,12 @@
     block = map_weight.shape[2]
     teacher_blocks, fan = map_dest.shape
     blocks = student_head.shape[1] // block
-    logits, all_s, all_id, peak_row = teacher_call(
+    logits, all_s, all_id, peak_row, peak_wide = teacher_call(
         chips, teacher_hidden, student_hidden, targets[None, :], teacher_head
     )
-    tokens = logits.shape[0]
-    weights = jnp.exp(logits - peak_row[0][:, None]).astype(jnp.bfloat16)
-    terms = jnp.einsum(
-        "gkc,krcd->krgd", weights.reshape(tokens, teacher_blocks, block), map_weight,
-        preferred_element_type=jnp.float32,
-    ).astype(jnp.bfloat16)
-    items = teacher_blocks * fan
-    goal = (map_dest * blocks + map_slot).reshape(items)
-    marks = (jnp.arange(places * blocks, dtype=jnp.int32)[:, None] == goal[None, :]).astype(jnp.bfloat16)
-    dense = jnp.dot(
-        marks, terms.reshape(items, tokens * block), preferred_element_type=jnp.float32
-    ).astype(jnp.bfloat16).reshape(places, blocks, tokens, block)
+    goal = (map_dest * blocks + map_slot).reshape(teacher_blocks * fan)
+    dense = map_call(goal, logits, peak_wide, map_weight, places * blocks)
+    dense = dense.reshape((places, blocks) + dense.shape[1:])
     return student_call(chips, vocabs, dense, peak_row, all_s, all_id, student_head)
 
 

time: 114 us -> 108 us (0.947)
  matrix products: 6.32 us -> 0 us
  Pallas kernels: 99.1 us -> 104 us
  local copies, waits for them, and re-layouts: 5.51 us -> 2.15 us
  other arithmetic: 2.39 us -> 0.7 us
    pallas_call x0 -> x1, Pallas kernels: none -> 9.08 us  [map_call(): pl.pallas_call(map_kernel, grid=(teacher_blocks // group,), out_shape=jax...]
    dot_general x2 -> x0, matrix products: 6.32 us -> none  [the longest x1 3.81 us: on_device(): jnp.einsum('gkc,krcd->krgd', weights.reshape(tokens, teacher_blocks, bloc...]
    unnamed x3 -> x1, local copies, waits for them, and re-layouts: 4.64 us -> 1.39 us
    pallas_call x1, Pallas kernels: 71.5 us -> 68.3 us  [student_call(): pl.pallas_call(functools.partial(student_kernel, chips, vocabs), out_shap...]
    unnamed x1 -> x0, other arithmetic: 1.68 us -> none
where the time goes in v3:
time: 108 us; the launch traced here: 107 us
  Pallas kernels  104 us (96%)
  local copies, waits for them, and re-layouts  2.15 us (2%)
    pallas_call x1, Pallas kernels, student_call(): pl.pallas_call(functools.partial(student_kernel, chips, vocabs), out_shap...  68.3 us
    pallas_call x1, Pallas kernels, teacher_call(): pl.pallas_call(functools.partial(teacher_kernel, chips), out_shape=(jax.S...  27.1 us
    pallas_call x1, Pallas kernels, map_call(): pl.pallas_call(map_kernel, grid=(teacher_blocks // group,), out_shape=jax...  9.08 us

profile of v3, /device:TPU:0, one launch (start us, length us, event | category | flops | bytes accessed | tf_op | source)
XLA Modules:
  0.0 107.3 jit_solution(2593734189354167894)
XLA Ops:
  0.0 0.7 multiply_add_fusion
  0.7 0.1 copy.9
  0.8 0.7 reshape.6.goal
  1.5 27.1 %shard_map.82 = (f32[64,6144]{1,0:T(8,128)}, bf16[8,8,4096]{2,1,0:T(8,128)(2,1)}, s32[8,8,128]{2,1,0:T(8,128)}, f32[8,64]{1,0:T(8,128)}, f32[64,128]{1,0:T(8,128)}) custom-call(bf16[8,5120]{1,0:T(8,128)(2,1)} %own_t.1, bf16[8,4096]{1,0:T(8,128)(2,1)} %own_s.1, s32[1,8]{1,0:T(1,128)} %bitcast.3, bf16[5120,6144]{1,0:T(8,128)(2,1)} %head.2), custom_call_target="tpu_custom_call" | custom-call | tf_op jit(solution)/shard_map/pallas_call | solution.py:150
  28.6 9.1 %shard_map.83 = bf16[256,64,128]{2,1,0:T(8,128)(2,1)} custom-call(s32[192]{0:T(256)} %reshape.6.goal, f32[64,6144]{1,0:T(8,128)} %get-tuple-element.10.logits, f32[64,128]{1,0:T(8,128)} %get-tuple-element.11.peak, bf16[48,4,128,128]{3,2,1,0:T(8,128)(2,1)} %weight.1), custom_call_target="tpu_custom_call" | custom-call | tf_op jit(solution)/shard_map/pallas_call | solution.py:213
  37.6 68.3 %shard_map.84 = bf16[4,4096]{1,0:T(4,128)(2,1)} custom-call(bf16[8,32,64,128]{3,2,1,0:T(8,128)(2,1)} %bitcast.2, f32[8,64]{1,0:T(8,128)} %get-tuple-element.12.peak_row, bf16[8,8,4096]{2,1,0:T(8,128)(2,1)} %get-tuple-element.13.all_s, s32[8,8,128]{2,1,0:T(8,128)} %get-tuple-element.14.all_id, bf16[4096,4096]{1,0:T(8,128)(2,1)} %head.3), custom_call_target="tpu_custom_call" | custom-call | tf_op jit(solution)/shard_map/pallas_call | solution.py:602
  105.9 1.4 %copy.11 = bf16[4,4096]{1,0:T(4,128)(2,1)} copy(bf16[4,4096]{1,0:T(4,128)(2,1)} %shard_map.84) | data formatting | bytes 65536
